TPU v7x, 32 devices: a whole 2x2x4 slice. The times are simulated.
32 devices in a mesh: front: 4 (over x, core), wide: 8 (over z, y).
Axes of the slice: x: 2, y: 2, z: 4, core: 2. Of those that a mesh axis runs over, the one named last changes fastest.
Arguments:
- inv_diag: bfloat16 [4, 8192, 8192], P('front', 'wide'), as said below
- below: bfloat16 [4, 6144, 8192], P('front', 'wide'), may hold values from -0.0625 to 0.0625
- rhs: bfloat16 [4, 8192, 256], P('front', 'wide'), may hold values from -6 to 6
- tile_count: int32 [4], replicated, may hold values from 36 to 48, as said below
- tile_owner: int32 [4, 48, 1], P('front', 'wide'), may hold values from 0 to 3; in each aligned block of 6 rows (0 to 5, 6 to 11, ..., all dimensions but the last counted through in order) at most 2 rows name the same one
- tile_rows: int32 [4, 48, 128], P('front', 'wide'), may hold values from 0 to 511
- parent_rhs: bfloat16 [4, 4096, 256], P('front', 'wide'), may hold values from -6 to 6
Outputs:
- solved: bfloat16 [4, 8192, 256], P('front', 'wide')
- parent_new: float32 [4, 4096, 256], P('front', 'wide')
Inputs may be any that keep to these rules, and one draw needn't show every extreme that they name: Each inv_diag[f] is lower triangular. Tiles of front f with index at least tile_count[f] carry nothing; some front has all 48 tiles live. `tile_owner`: among the 6 tiles of one device (aligned blocks of tiles), no front index is named more than 2 times.
All inputs are finite; a program needn't handle non-finite values.
Results may differ from a plain program's by a relative error of at most 0.0037.
Values may be sent and summed in bfloat16 or wider, within the bound.
No kernel may reach another device: no remote copies, remote signals or barrier semaphores. Data moves between devices by JAX's collectives and lax.ppermute only.
A program may use at most 128 MiB of HBM per device.

v0:
```python
import jax
import jax.numpy as jnp
from jax import lax
from jax.sharding import PartitionSpec as P

CAPACITY = 2


def body(inv_diag, below, rhs, tile_count, tile_owner, tile_rows, parent_rhs):
    inv_rows = inv_diag[0]
    below_rows = below[0]
    rhs_rows = rhs[0]
    rhs_width = rhs_rows.shape[1]
    gathered = lax.all_gather(rhs_rows, "wide", axis=0, tiled=True)
    solved = jnp.dot(inv_rows, gathered, preferred_element_type=jnp.float32).astype(jnp.bfloat16)
    solved_all = lax.all_gather(solved, "wide", axis=0, tiled=True)
    update_rows = jnp.dot(below_rows, solved_all, preferred_element_type=jnp.float32)
    tiles_here = tile_owner.shape[1]
    tile_height = tile_rows.shape[2]
    parent_height = parent_rhs.shape[1]
    group_index = lax.axis_index("front")
    wide_index = lax.axis_index("wide")
    count_live = lax.dynamic_index_in_dim(tile_count, group_index, 0, keepdims=False)
    numbers = wide_index * tiles_here + jnp.arange(tiles_here, dtype=jnp.int32)
    alive = numbers < count_live
    update_tiles = update_rows.astype(jnp.bfloat16).reshape(tiles_here, tile_height, rhs_width)
    update_tiles = jnp.where(alive[:, None, None], update_tiles, jnp.zeros_like(update_tiles))
    targets = jnp.where(alive[:, None], tile_rows[0], parent_height)
    owners = tile_owner[0, :, 0]
    front_count = lax.axis_size("front")
    slot_count = CAPACITY
    serial = jnp.arange(tiles_here, dtype=jnp.int32)
    same_owner = owners[:, None] == owners[None, :]
    earlier = serial[None, :] < serial[:, None]
    slot_index = jnp.sum((same_owner & earlier).astype(jnp.int32), axis=1)
    slot_place = owners * slot_count + slot_index
    chooser = jnp.arange(front_count * slot_count, dtype=jnp.int32)[:, None] == slot_place[None, :]
    tile_values = jnp.dot(
        chooser.astype(jnp.bfloat16),
        update_tiles.reshape(tiles_here, tile_height * rhs_width),
        preferred_element_type=jnp.float32,
    )
    tile_values = tile_values.astype(jnp.bfloat16).reshape(
        front_count, slot_count, tile_height, rhs_width
    )
    occupied = jnp.any(chooser, axis=1)
    picked_rows = jnp.sum(chooser.astype(jnp.int32)[:, :, None] * targets[None, :, :], axis=1)
    rows_sent = jnp.where(occupied[:, None], picked_rows, parent_height)
    rows_sent = rows_sent.reshape(front_count, slot_count, tile_height)
    arrived_values, arrived_rows = (
        lax.all_to_all(tile_values, "front", split_axis=0, concat_axis=0, tiled=True),
        lax.all_to_all(rows_sent, "front", split_axis=0, concat_axis=0, tiled=True),
    )
    flat_values = arrived_values.reshape(-1, rhs_width)
    flat_rows = arrived_rows.reshape(-1)
    placement_hits = (
        jnp.arange(parent_height, dtype=jnp.int32)[:, None] == flat_rows[None, :]
    ).astype(jnp.bfloat16)
    incoming = jnp.dot(placement_hits, flat_values, preferred_element_type=jnp.float32)
    parent_new = parent_rhs[0].astype(jnp.float32) - incoming
    return (solved[None], parent_new[None])


def solution(mesh):
    return jax.shard_map(
        body,
        mesh=mesh,
        in_specs=(
            P("front", "wide", None),
            P("front", "wide", None),
            P("front", "wide", None),
            P(),
            P("front", "wide", None),
            P("front", "wide", None),
            P("front", "wide", None),
        ),
        out_specs=(P("front", "wide", None), P("front", "wide", None)),
        check_vma=False,
    )
```

profile of v0, /device:TPU:0, one launch (start us, length us, event | category | flops | bytes accessed | tf_op | source)
XLA Modules:
  0.0 200.3 jit_solution(4259443388356019072)
XLA Ops:
  7.2 0.0 all-gather.6.cloned.1.call-start
  7.2 0.7 all-gather.6.cloned.1.call-update
  7.9 0.0 copy-start.2
  7.9 0.0 copy-start
  7.9 0.0 copy-start.3
  7.9 0.0 all-gather.4.cloned.1.call-start
  8.0 78.3 %all-gather.6.cloned.1.call-done = bf16[1,8192,256]{2,1,0:T(8,128)(2,1)} async-done(((bf16[1,1024,256]{2,1,0:T(8,128)(2,1)}), bf16[1,8192,256]{2,1,0:T(8,128)(2,1)}) %all-gather.6.cloned.1.call-update) | async-done | bytes 4194320 | tf_op jit(solution)/shard_map/all_gather | solution.py:14
  86.3 12.2 %fusion.6 = bf16[1024,256]{1,0:T(8,128)(2,1)} fusion(bf16[1,8192,256]{2,1,0:T(8,128)(2,1)} %all-gather.6.cloned.1.call-done, bf16[1,1024,8192]{2,1,0:T(8,128)(2,1)} %param.7), kind=kOutput, calls=%fused_computation.8 | convolution fusion | flops 4295229440 | bytes 21495808 | tf_op jit(solution)/shard_map/dot_general | solution.py:15
  98.5 0.0 all-gather.4.cloned.1.call-update
  98.5 0.0 copy-done.2
  98.5 0.6 dynamic_slice.4
  99.1 0.7 add_compare_fusion
  99.8 0.0 copy-done
  99.8 0.1 broadcast_select_fusion
  99.9 0.0 copy-done.3
  99.9 0.2 convert_reduce_fusion
  100.1 0.1 fusion.24
  100.2 0.1 copy.10
  100.3 0.1 broadcast_in_dim.54
  100.3 0.1 multiply_reduce_fusion
  100.4 0.7 broadcast_select_fusion.1
  101.1 3.2 %all-to-all-start = ((s32[4,2,128]{2,1,0:T(2,128)}), s32[4,2,128]{2,1,0:T(2,128)S(1)}, u32[]{:S(2)}, u32[]{:S(2)}) async-start(s32[4,2,128]{2,1,0:T(2,128)} %broadcast_select_fusion.1), calls=%async_computation | async-start | bytes 8192 | tf_op jit(solution)/shard_map/all_to_all | solution.py:52
  104.4 66.0 %all-gather.4.cloned.1.call-done = bf16[8192,256]{1,0:T(8,128)(2,1)} async-done(((bf16[1024,256]{1,0:T(8,128)(2,1)}), bf16[8192,256]{1,0:T(8,128)(2,1)}) %all-gather.4.cloned.1.call-update) | async-done | bytes 4194320 | tf_op jit(solution)/shard_map/all_gather | solution.py:16
  170.3 9.3 %fusion.16 = bf16[768,256]{0,1:T(8,128)(2,1)S(1)} fusion(bf16[8192,256]{1,0:T(8,128)(2,1)} %all-gather.4.cloned.1.call-done, bf16[1,768,8192]{2,1,0:T(8,128)(2,1)} %param.8), kind=kOutput, calls=%fused_computation.12 | convolution fusion | flops 3221422080 | bytes 17170432 | tf_op jit(solution)/shard_map/dot_general | solution.py:17
  179.7 0.0 copy-start.1
  179.7 0.2 copy.11
  179.9 0.4 reshape.73
  180.3 0.4 convolution_convert_fusion
  180.6 0.1 copy.13
  180.8 0.0 all-to-all-done
  180.8 11.4 %all_to_all.10 = bf16[4,2,128,256]{3,2,1,0:T(8,128)(2,1)S(1)} all-to-all(bf16[4,2,128,256]{3,2,1,0:T(8,128)(2,1)S(1)} %bitcast.40), channel_id=1, replica_groups=mesh['front'=4,'wide'=8] {'front'}, dimensions={0} | all-to-all | bytes 1048576 | tf_op jit(solution)/shard_map/all_to_all | solution.py:51
  192.2 0.0 copy-done.1
  192.2 1.3 fusion.15
  (2 shorter events, 0.0 us)
Async XLA Ops:
  7.2 79.1 %all-gather.6.cloned.1.call-start = ((), (), s32[]{:S(2)}) async-start(), calls=%async_computation.3 | async-start | bytes 4718592 | tf_op jit(solution)/shard_map/all_gather | solution.py:14
  7.9 90.6 %copy-start.2 = (s32[4]{0:T(128)S(1)}, s32[4]{0:T(128)}, u32[]{:S(2)}) copy-start(s32[4]{0:T(128)} %param.10) | copy-start | bytes 52
  7.9 91.9 %copy-start = (s32[1,6,128]{2,0,1:T(1,128)S(1)}, s32[1,6,128]{2,0,1:T(1,128)}, u32[]{:S(2)}) copy-start(s32[1,6,128]{2,0,1:T(1,128)} %param.12) | copy-start | bytes 9220
  7.9 92.0 %copy-start.3 = (s32[1,6,1]{1,2,0:T(1,128)S(1)}, s32[1,6,1]{1,2,0:T(1,128)}, u32[]{:S(2)}) copy-start(s32[1,6,1]{1,2,0:T(1,128)} %param.11) | copy-start | bytes 76
  7.9 162.4 %all-gather.4.cloned.1.call-start = ((), (), s32[]{:S(2)}) async-start(), calls=%async_computation.2 | async-start | bytes 4718592 | tf_op jit(solution)/shard_map/all_gather | solution.py:16
  101.1 79.7 %all-to-all-start = ((s32[4,2,128]{2,1,0:T(2,128)}), s32[4,2,128]{2,1,0:T(2,128)S(1)}, u32[]{:S(2)}, u32[]{:S(2)}) async-start(s32[4,2,128]{2,1,0:T(2,128)} %broadcast_select_fusion.1), calls=%async_computation | async-start | bytes 8192 | tf_op jit(solution)/shard_map/all_to_all | solution.py:52
  179.7 12.5 %copy-start.1 = (bf16[1,512,256]{2,1,0:T(8,128)(2,1)S(1)}, bf16[1,512,256]{2,1,0:T(8,128)(2,1)}, u32[]{:S(2)}) copy-start(bf16[1,512,256]{2,1,0:T(8,128)(2,1)} %param.13) | copy-start | bytes 786436
Sparse Core Ops, SparseCore 0:
  10.1 76.0 all-gather.5
  98.6 71.6 all-gather.3
where the time goes:
time: 200 us
  waiting for transfers between devices  145 us (72%)
  matrix products  23.2 us (12%)
  between operations  14.2 us (7%)
  blocking collectives  11.4 us (6%)
  starting transfers between devices  3.32 us (2%)
    all_gather x1, waiting for transfers between devices, body(): gathered = lax.all_gather(rhs_rows, 'wide', axis=0, tiled=True)  78.3 us
    all_gather x1, waiting for transfers between devices, body(): solved_all = lax.all_gather(solved, 'wide', axis=0, tiled=True)  66 us
    dot_general x1, matrix products, body(): jnp.dot(inv_rows, gathered, preferred_element_type=jnp.float32)  12.2 us
    all_to_all x1, blocking collectives, body(): lax.all_to_all(tile_values, 'front', split_axis=0, concat_axis=0, tiled=T...  11.4 us
    dot_general x1, matrix products, body(): jnp.dot(below_rows, solved_all, preferred_element_type=jnp.float32)  9.32 us
  transfers between devices with their start and end apart: 3, of which 2 were waited for; matrix products, arithmetic and copies ran while one was open for 6% of the time, Pallas kernels for 0%

commit v1 on v0

v1 whole, which is shorter than its diff:
```python
import jax
import jax.numpy as jnp
from jax import lax
from jax.sharding import PartitionSpec as P

CAPACITY = 2


def ring_order(count):
    if count % 8:
        return list(range(count))
    depth = 4
    columns = count // depth
    walk = [z * columns for z in range(depth)]
    for step, z in enumerate(range(depth - 1, -1, -1)):
        ys = range(1, columns) if step % 2 == 0 else range(columns - 1, 0, -1)
        walk += [z * columns + y for y in ys]
    return walk


def lookup(table, index):
    result = jnp.int32(table[0])
    for place in range(1, len(table)):
        result = jnp.where(index == place, jnp.int32(table[place]), result)
    return result


def dot(a, b):
    return jnp.dot(a, b, preferred_element_type=jnp.float32)


def ring_product(matrix, block, order, place):
    count = len(order)
    rows = block.shape[0]
    half = rows // 2
    onward = [(order[i], order[(i + 1) % count]) for i in range(count)]
    backward = [(b, a) for a, b in onward]

    def part(index, offset, values):
        columns = lax.dynamic_slice_in_dim(matrix, index * rows + offset, values.shape[0], 1)
        return dot(columns, values)

    first, second = block[:half], block[half:]
    total = part(lookup(order, place), 0, block)
    for step in range(1, count):
        first = lax.ppermute(first, "wide", onward)
        second = lax.ppermute(second, "wide", backward)
        from_left = lookup(order, (place + count - step) % count)
        from_right = lookup(order, (place + step) % count)
        total = total + part(from_left, 0, first)
        total = total + part(from_right, half, second)
    return total


def body(inv_diag, below, rhs, tile_count, tile_owner, tile_rows, parent_rhs):
    width = rhs.shape[2]
    tiles = tile_owner.shape[1]
    height = tile_rows.shape[2]
    parent_height = parent_rhs.shape[1]
    fronts = lax.axis_size("front")
    wide = lax.axis_size("wide")
    me = lax.axis_index("front")
    wide_index = lax.axis_index("wide")
    order = ring_order(wide)
    place = lookup([order.index(i) for i in range(wide)], wide_index)

    serial = jnp.arange(tiles, dtype=jnp.int32)
    live_count = jnp.sum(jnp.where(jnp.arange(fronts) == me, tile_count, 0))
    alive = wide_index * tiles + serial < live_count
    owners = tile_owner[0, :, 0]
    same_owner = owners[:, None] == owners[None, :]
    earlier = serial[None, :] < serial[:, None]
    slot = jnp.sum((same_owner & earlier).astype(jnp.int32), axis=1)
    targets = jnp.where(alive[:, None], tile_rows[0], parent_height)

    def chooser_for(owner):
        return (owners[None, :] == owner) & (slot[None, :] == jnp.arange(CAPACITY)[:, None])

    choosers = [chooser_for(me ^ delta) for delta in range(fronts)]
    rows_out = [
        jnp.where(
            jnp.any(c, axis=1)[:, None],
            jnp.sum(jnp.where(c[:, :, None], targets[None], 0), axis=1),
            parent_height,
        )
        for c in choosers
    ]
    swaps = [[(i, i ^ delta) for i in range(fronts)] for delta in range(fronts)]
    rows_in = [rows_out[0]] + [
        lax.ppermute(rows_out[delta], "front", swaps[delta]) for delta in range(1, fronts)
    ]

    solved = ring_product(inv_diag[0], rhs[0], order, place).astype(jnp.bfloat16)
    update = ring_product(below[0], solved, order, place).astype(jnp.bfloat16)
    update = update.reshape(tiles, height, width)
    update = jnp.where(alive[:, None, None], update, jnp.zeros_like(update))
    flat = update.reshape(tiles, height * width)
    values_out = [
        dot(c.astype(jnp.bfloat16), flat).astype(jnp.bfloat16).reshape(CAPACITY * height, width)
        for c in choosers
    ]
    values_in = [values_out[0]] + [
        lax.ppermute(values_out[delta], "front", swaps[delta]) for delta in range(1, fronts)
    ]
    parent_new = parent_rhs[0].astype(jnp.float32)
    numbers = jnp.arange(parent_height, dtype=jnp.int32)[:, None]
    for rows, values in zip(rows_in, values_in):
        hits = (numbers == rows.reshape(1, -1)).astype(jnp.bfloat16)
        parent_new = parent_new - dot(hits, values)
    return (solved[None], parent_new[None])


def solution(mesh):
    split = P("front", "wide", None)
    return jax.shard_map(
        body,
        mesh=mesh,
        in_specs=(split, split, split, P(), split, split, split),
        out_specs=(split, split),
        check_vma=False,
    )
```

time: 200 us -> 131 us (0.66)
  waiting for transfers between devices: 145 us -> 63.3 us
  starting transfers between devices: 3.32 us -> 36 us
  between operations: 14.2 us -> 1.25 us
  blocking collectives: 11.4 us -> 0 us
  other arithmetic: 1.78 us -> 4.82 us
    all_gather x2 -> x0, waiting for transfers between devices: 144 us -> none  [the longest x1 78.3 us: body(): gathered = lax.all_gather(rhs_rows, 'wide', axis=0, tiled=True)]
    ppermute x0 -> x34, waiting for transfers between devices: none -> 63.3 us  [the longest x14 43.4 us: ring_product(): second = lax.ppermute(second, 'wide', backward)]
    ppermute x0 -> x34, starting transfers between devices: none -> 36 us  [the longest x14 23.1 us: ring_product(): second = lax.ppermute(second, 'wide', backward)]
    all_to_all x1 -> x0, blocking collectives: 11.4 us -> none  [body(): lax.all_to_all(tile_values, 'front', split_axis=0, concat_axis=0, tiled=T...]
    all_to_all x1 -> x0, starting transfers between devices: 3.25 us -> none  [body(): lax.all_to_all(rows_sent, 'front', split_axis=0, concat_axis=0, tiled=True)]
    reduce_sum x2 -> x3, other arithmetic: 0.26 us -> 2.31 us  [the longest x1 1.29 us: body(): live_count = jnp.sum(jnp.where(jnp.arange(fronts) == me, tile_count, 0))]
    dot_general x4 -> x38, matrix products: 23.2 us -> 23.2 us  [dot(): return jnp.dot(a, b, preferred_element_type=jnp.float32)]
  transfers between devices with their start and end apart: 3 -> 34, of which waited for: 2 -> 23; matrix products, arithmetic and copies ran while one was open for 6% -> 22% of each run, Pallas kernels for 0% -> 0%
where the time goes in v1:
time: 131 us
  waiting for transfers between devices  63.3 us (48%)
  starting transfers between devices  36 us (27%)
  matrix products  23.2 us (18%)
  other arithmetic  4.82 us (4%)
  local copies, waits for them, and re-layouts  2.36 us (2%)
    ppermute x14, waiting for transfers between devices, ring_product(): second = lax.ppermute(second, 'wide', backward)  43.4 us
    dot_general x38, matrix products, dot(): return jnp.dot(a, b, preferred_element_type=jnp.float32)  23.2 us
    ppermute x14, starting transfers between devices, ring_product(): second = lax.ppermute(second, 'wide', backward)  23.1 us
    ppermute x14, waiting for transfers between devices, ring_product(): first = lax.ppermute(first, 'wide', onward)  15.5 us
    ppermute x14, starting transfers between devices, ring_product(): first = lax.ppermute(first, 'wide', onward)  8.42 us
    ppermute x3, waiting for transfers between devices, body(): lax.ppermute(values_out[delta], 'front', swaps[delta])  4.37 us
  transfers between devices with their start and end apart: 34, of which 23 were waited for; matrix products, arithmetic and copies ran while one was open for 22% of the time, Pallas kernels for 0%

profile of v1, /device:TPU:0, one launch (start us, length us, event | category | flops | bytes accessed | tf_op | source)
XLA Modules:
  0.0 130.9 jit_solution(2408351855697931282)
XLA Ops:
  0.6 1.1 slice_bitcast_fusion.1
  1.7 3.1 %collective-permute-start = (bf16[512,256]{1,0:T(8,128)(2,1)S(1)}, bf16[512,256]{1,0:T(8,128)(2,1)S(1)}, u32[]{:S(2)}, u32[]{:S(2)}) collective-permute-start(bf16[512,256]{1,0:T(8,128)(2,1)S(1)} %get-tuple-element.16), channel_id=1, source_target_pairs={{0,2},{2,4},{4,6},{6,7},{7,5},{5,3},{3,1},{1,0},{8,10},{10,12},{12... | collective-permute-start | bytes 786440 | tf_op jit(solution)/shard_map/ppermute | solution.py:46
  4.8 0.9 convert_reduce_fusion
  5.7 1.3 fusion.133
  7.0 0.7 broadcast_compare_fusion.3
  8.2 0.7 add_compare_fusion
  8.9 0.8 broadcast_select_fusion.1
  9.8 1.9 %collective-permute-start.30 = (s32[2,128]{1,0:T(2,128)S(1)}, s32[2,128]{1,0:T(2,128)S(1)}, u32[]{:S(2)}, u32[]{:S(2)}) collective-permute-start(s32[2,128]{1,0:T(2,128)S(1)} %broadcast_select_fusion.3), channel_id=1, source_target_pairs={{0,16},{8,24},{16,0},{24,8},{1,17},{9,25},{17,1},{25,9},{2,18},{10... | collective-permute-start | bytes 3080 | tf_op jit(solution)/shard_map/ppermute | solution.py:90
  12.3 2.5 %fusion = f32[1024,256]{1,0:T(8,128)S(1)} fusion(bf16[1,1024,8192]{2,1,0:T(8,128)(2,1)} %param.7, s32[]{:T(128)S(6)} %select_n.537, bf16[1,1024,256]{2,1,0:T(8,128)(2,1)} %param.9), kind=kOutput, calls=%fused_computation.4 | convolution fusion | flops 536870912 | bytes 3670020 | tf_op jit(solution)/shard_map/dot_general | solution.py:29
  14.8 1.9 %collective-permute-start.3 = (bf16[512,256]{1,0:T(8,128)(2,1)S(1)}, bf16[512,256]{1,0:T(8,128)(2,1)S(1)}, u32[]{:S(2)}, u32[]{:S(2)}) collective-permute-start(bf16[512,256]{1,0:T(8,128)(2,1)S(1)} %collective-permute-done.1), channel_id=1, source_target_pairs={{2,0},{4,2},{6,4},{7,6},{5,7},{3,5},{1,3},{0,1},{10,8},{12,10},{14... | collective-permute-start | bytes 786440 | tf_op jit(solution)/shard_map/ppermute | solution.py:47
  16.9 2.4 %convolution_add_fusion.7 = f32[1024,256]{1,0:T(8,128)S(1)} fusion(f32[1024,256]{1,0:T(8,128)S(1)} %fusion, bf16[512,256]{1,0:T(8,128)(2,1)S(1)} %collective-permute-done, bf16[1,1024,8192]{2,1,0:T(8,128)(2,1)} %param.7, s32[]{:T(128)S(6)} %select_n.546), kind=kOutput, calls=%fused_computation.23 | convolution fusion | flops 268697600 | bytes 3407876 | tf_op jit(solution)/shard_map/dot_general | solution.py:29
  19.3 1.7 %convolution_add_fusion.6 = f32[1024,256]{1,0:T(8,128)S(1)} fusion(f32[1024,256]{1,0:T(8,128)S(1)} %convolution_add_fusion.7, bf16[512,256]{1,0:T(8,128)(2,1)S(1)} %collective-permute-done.1, bf16[1,1024,8192]{2,1,0:T(8,128)(2,1)} %param.7, s32[]{:T(128)S(6)} %select_n.555), kind=kOutput, calls=%fused_computation.22 | convolution fusion | flops 268697600 | bytes 3407876 | tf_op jit(solution)/shard_map/dot_general | solution.py:29
  21.0 2.3 %collective-permute-done.3 = bf16[512,256]{1,0:T(8,128)(2,1)S(1)} collective-permute-done((bf16[512,256]{1,0:T(8,128)(2,1)S(1)}, bf16[512,256]{1,0:T(8,128)(2,1)S(1)}, u32[]{:S(2)}, u32[]{:S(2)}) %collective-permute-start.3) | collective-permute-done | bytes 262176 | tf_op jit(solution)/shard_map/ppermute | solution.py:47
  23.3 1.7 %collective-permute-start.5 = (bf16[512,256]{1,0:T(8,128)(2,1)S(1)}, bf16[512,256]{1,0:T(8,128)(2,1)S(1)}, u32[]{:S(2)}, u32[]{:S(2)}) collective-permute-start(bf16[512,256]{1,0:T(8,128)(2,1)S(1)} %collective-permute-done.3), channel_id=1, source_target_pairs={{2,0},{4,2},{6,4},{7,6},{5,7},{3,5},{1,3},{0,1},{10,8},{12,10},{14... | collective-permute-start | bytes 786440 | tf_op jit(solution)/shard_map/ppermute | solution.py:47
  24.9 1.7 %fusion.38 = f32[1024,256]{1,0:T(8,128)S(1)} fusion(bf16[512,256]{1,0:T(8,128)(2,1)S(1)} %collective-permute-done.3, bf16[1,1024,8192]{2,1,0:T(8,128)(2,1)} %param.7, s32[]{:T(128)S(6)} %select_n.573), kind=kOutput, calls=%fused_computation.60 | convolution fusion | flops 268435456 | bytes 2359300 | tf_op jit(solution)/shard_map/dot_general | solution.py:29
  27.0 1.7 %fusion.11 = f32[1024,256]{1,0:T(8,128)S(1)} fusion(f32[1024,256]{1,0:T(8,128)S(1)} %fusion.38, f32[1024,256]{1,0:T(8,128)S(1)} %convolution_add_fusion.6, bf16[512,256]{1,0:T(8,128)(2,1)S(1)} %collective-permute-done.2, bf16[1,1024,8192]{2,1,0:T(8,128)(2,1)} %param.7, s32[]{:T(128)S(6)} %select_n.564), kind=kOutput, calls=%fused_computation.21 | convolution fusion | flops 268959744 | bytes 4456452 | tf_op jit(solution)/shard_map/dot_general | solution.py:29
  28.7 2.2 %collective-permute-done.5 = bf16[512,256]{1,0:T(8,128)(2,1)S(1)} collective-permute-done((bf16[512,256]{1,0:T(8,128)(2,1)S(1)}, bf16[512,256]{1,0:T(8,128)(2,1)S(1)}, u32[]{:S(2)}, u32[]{:S(2)}) %collective-permute-start.5) | collective-permute-done | bytes 262176 | tf_op jit(solution)/shard_map/ppermute | solution.py:47
  30.8 1.4 %collective-permute-start.7 = (bf16[512,256]{1,0:T(8,128)(2,1)S(1)}, bf16[512,256]{1,0:T(8,128)(2,1)S(1)}, u32[]{:S(2)}, u32[]{:S(2)}) collective-permute-start(bf16[512,256]{1,0:T(8,128)(2,1)S(1)} %collective-permute-done.5), channel_id=1, source_target_pairs={{2,0},{4,2},{6,4},{7,6},{5,7},{3,5},{1,3},{0,1},{10,8},{12,10},{14... | collective-permute-start | bytes 786440 | tf_op jit(solution)/shard_map/ppermute | solution.py:47
  32.7 1.0 collective-permute-done.4
  33.7 0.6 collective-permute-start.6
  34.3 0.4 fusion.10
  34.7 2.7 %collective-permute-done.7 = bf16[512,256]{1,0:T(8,128)(2,1)S(1)} collective-permute-done((bf16[512,256]{1,0:T(8,128)(2,1)S(1)}, bf16[512,256]{1,0:T(8,128)(2,1)S(1)}, u32[]{:S(2)}, u32[]{:S(2)}) %collective-permute-start.7) | collective-permute-done | bytes 262176 | tf_op jit(solution)/shard_map/ppermute | solution.py:47
  37.5 1.6 %collective-permute-start.9 = (bf16[512,256]{1,0:T(8,128)(2,1)S(1)}, bf16[512,256]{1,0:T(8,128)(2,1)S(1)}, u32[]{:S(2)}, u32[]{:S(2)}) collective-permute-start(bf16[512,256]{1,0:T(8,128)(2,1)S(1)} %collective-permute-done.7), channel_id=1, source_target_pairs={{2,0},{4,2},{6,4},{7,6},{5,7},{3,5},{1,3},{0,1},{10,8},{12,10},{14... | collective-permute-start | bytes 786440 | tf_op jit(solution)/shard_map/ppermute | solution.py:47
  39.0 0.4 fusion.32
  39.5 0.9 collective-permute-done.6
  40.7 0.4 fusion.9
  41.2 3.4 %collective-permute-done.9 = bf16[512,256]{1,0:T(8,128)(2,1)S(1)} collective-permute-done((bf16[512,256]{1,0:T(8,128)(2,1)S(1)}, bf16[512,256]{1,0:T(8,128)(2,1)S(1)}, u32[]{:S(2)}, u32[]{:S(2)}) %collective-permute-start.9) | collective-permute-done | bytes 262176 | tf_op jit(solution)/shard_map/ppermute | solution.py:47
  44.6 1.9 %collective-permute-start.11 = (bf16[512,256]{1,0:T(8,128)(2,1)S(1)}, bf16[512,256]{1,0:T(8,128)(2,1)S(1)}, u32[]{:S(2)}, u32[]{:S(2)}) collective-permute-start(bf16[512,256]{1,0:T(8,128)(2,1)S(1)} %collective-permute-done.9), channel_id=1, source_target_pairs={{2,0},{4,2},{6,4},{7,6},{5,7},{3,5},{1,3},{0,1},{10,8},{12,10},{14... | collective-permute-start | bytes 786440 | tf_op jit(solution)/shard_map/ppermute | solution.py:47
  46.5 0.4 fusion.29
  47.0 0.8 collective-permute-done.8
  47.9 0.4 fusion.8
  48.3 4.2 %collective-permute-done.11 = bf16[512,256]{1,0:T(8,128)(2,1)S(1)} collective-permute-done((bf16[512,256]{1,0:T(8,128)(2,1)S(1)}, bf16[512,256]{1,0:T(8,128)(2,1)S(1)}, u32[]{:S(2)}, u32[]{:S(2)}) %collective-permute-start.11) | collective-permute-done | bytes 262176 | tf_op jit(solution)/shard_map/ppermute | solution.py:47
  52.5 2.4 %collective-permute-start.13 = (bf16[512,256]{1,0:T(8,128)(2,1)S(1)}, bf16[512,256]{1,0:T(8,128)(2,1)S(1)}, u32[]{:S(2)}, u32[]{:S(2)}) collective-permute-start(bf16[512,256]{1,0:T(8,128)(2,1)S(1)} %collective-permute-done.11), channel_id=1, source_target_pairs={{2,0},{4,2},{6,4},{7,6},{5,7},{3,5},{1,3},{0,1},{10,8},{12,10},{14... | collective-permute-start | bytes 786440 | tf_op jit(solution)/shard_map/ppermute | solution.py:47
  54.9 0.4 fusion.26
  55.3 0.7 collective-permute-done.10
  56.0 0.4 fusion.7
  56.5 2.6 %collective-permute-done.13 = bf16[512,256]{1,0:T(8,128)(2,1)S(1)} collective-permute-done((bf16[512,256]{1,0:T(8,128)(2,1)S(1)}, bf16[512,256]{1,0:T(8,128)(2,1)S(1)}, u32[]{:S(2)}, u32[]{:S(2)}) %collective-permute-start.13) | collective-permute-done | bytes 262176 | tf_op jit(solution)/shard_map/ppermute | solution.py:47
  59.1 0.4 fusion.23
  59.6 5.1 %collective-permute-done.12 = bf16[512,256]{1,0:T(8,128)(2,1)S(1)} collective-permute-done((bf16[512,256]{1,0:T(8,128)(2,1)S(1)}, bf16[512,256]{1,0:T(8,128)(2,1)S(1)}, u32[]{:S(2)}, u32[]{:S(2)}) %collective-permute-start.12) | collective-permute-done | bytes 262176 | tf_op jit(solution)/shard_map/ppermute | solution.py:46
  64.7 0.4 fusion.12
  65.3 2.0 %collective-permute-start.15 = (bf16[512,256]{1,0:T(8,128)(2,1)S(1)}, bf16[512,256]{1,0:T(8,128)(2,1)S(1)}, u32[]{:S(2)}, u32[]{:S(2)}) collective-permute-start(bf16[512,256]{1,0:T(8,128)(2,1)S(1)} %get-tuple-element.15), channel_id=1, source_target_pairs={{2,0},{4,2},{6,4},{7,6},{5,7},{3,5},{1,3},{0,1},{10,8},{12,10},{14... | collective-permute-start | bytes 786440 | tf_op jit(solution)/shard_map/ppermute | solution.py:47
  67.3 0.6 fusion.3
  67.9 5.3 %collective-permute-done.14 = bf16[512,256]{1,0:T(8,128)(2,1)S(1)} collective-permute-done((bf16[512,256]{1,0:T(8,128)(2,1)S(1)}, bf16[512,256]{1,0:T(8,128)(2,1)S(1)}, u32[]{:S(2)}, u32[]{:S(2)}) %collective-permute-start.14) | collective-permute-done | bytes 262176 | tf_op jit(solution)/shard_map/ppermute | solution.py:46
  73.9 1.8 %collective-permute-start.17 = (bf16[512,256]{1,0:T(8,128)(2,1)S(1)}, bf16[512,256]{1,0:T(8,128)(2,1)S(1)}, u32[]{:S(2)}, u32[]{:S(2)}) collective-permute-start(bf16[512,256]{1,0:T(8,128)(2,1)S(1)} %collective-permute-done.15), channel_id=1, source_target_pairs={{2,0},{4,2},{6,4},{7,6},{5,7},{3,5},{1,3},{0,1},{10,8},{12,10},{14... | collective-permute-start | bytes 786440 | tf_op jit(solution)/shard_map/ppermute | solution.py:47
  76.1 5.3 %collective-permute-done.17 = bf16[512,256]{1,0:T(8,128)(2,1)S(1)} collective-permute-done((bf16[512,256]{1,0:T(8,128)(2,1)S(1)}, bf16[512,256]{1,0:T(8,128)(2,1)S(1)}, u32[]{:S(2)}, u32[]{:S(2)}) %collective-permute-start.17) | collective-permute-done | bytes 262176 | tf_op jit(solution)/shard_map/ppermute | solution.py:47
  81.4 1.3 collective-permute-start.19
  83.1 0.8 collective-permute-start.18
  84.3 3.7 %collective-permute-done.19 = bf16[512,256]{1,0:T(8,128)(2,1)S(1)} collective-permute-done((bf16[512,256]{1,0:T(8,128)(2,1)S(1)}, bf16[512,256]{1,0:T(8,128)(2,1)S(1)}, u32[]{:S(2)}, u32[]{:S(2)}) %collective-permute-start.19) | collective-permute-done | bytes 262176 | tf_op jit(solution)/shard_map/ppermute | solution.py:47
  87.9 1.8 %collective-permute-start.21 = (bf16[512,256]{1,0:T(8,128)(2,1)S(1)}, bf16[512,256]{1,0:T(8,128)(2,1)S(1)}, u32[]{:S(2)}, u32[]{:S(2)}) collective-permute-start(bf16[512,256]{1,0:T(8,128)(2,1)S(1)} %collective-permute-done.19), channel_id=1, source_target_pairs={{2,0},{4,2},{6,4},{7,6},{5,7},{3,5},{1,3},{0,1},{10,8},{12,10},{14... | collective-permute-start | bytes 786440 | tf_op jit(solution)/shard_map/ppermute | solution.py:47
  90.5 0.6 collective-permute-start.20
  91.4 4.0 %collective-permute-done.21 = bf16[512,256]{1,0:T(8,128)(2,1)S(1)} collective-permute-done((bf16[512,256]{1,0:T(8,128)(2,1)S(1)}, bf16[512,256]{1,0:T(8,128)(2,1)S(1)}, u32[]{:S(2)}, u32[]{:S(2)}) %collective-permute-start.21) | collective-permute-done | bytes 262176 | tf_op jit(solution)/shard_map/ppermute | solution.py:47
  95.4 2.1 %collective-permute-start.23 = (bf16[512,256]{1,0:T(8,128)(2,1)S(1)}, bf16[512,256]{1,0:T(8,128)(2,1)S(1)}, u32[]{:S(2)}, u32[]{:S(2)}) collective-permute-start(bf16[512,256]{1,0:T(8,128)(2,1)S(1)} %collective-permute-done.21), channel_id=1, source_target_pairs={{2,0},{4,2},{6,4},{7,6},{5,7},{3,5},{1,3},{0,1},{10,8},{12,10},{14... | collective-permute-start | bytes 786440 | tf_op jit(solution)/shard_map/ppermute | solution.py:47
  98.5 5.9 %collective-permute-done.23 = bf16[512,256]{1,0:T(8,128)(2,1)S(1)} collective-permute-done((bf16[512,256]{1,0:T(8,128)(2,1)S(1)}, bf16[512,256]{1,0:T(8,128)(2,1)S(1)}, u32[]{:S(2)}, u32[]{:S(2)}) %collective-permute-start.23) | collective-permute-done | bytes 262176 | tf_op jit(solution)/shard_map/ppermute | solution.py:47
  104.5 2.0 %collective-permute-start.25 = (bf16[512,256]{1,0:T(8,128)(2,1)S(1)}, bf16[512,256]{1,0:T(8,128)(2,1)S(1)}, u32[]{:S(2)}, u32[]{:S(2)}) collective-permute-start(bf16[512,256]{1,0:T(8,128)(2,1)S(1)} %collective-permute-done.23), channel_id=1, source_target_pairs={{2,0},{4,2},{6,4},{7,6},{5,7},{3,5},{1,3},{0,1},{10,8},{12,10},{14... | collective-permute-start | bytes 786440 | tf_op jit(solution)/shard_map/ppermute | solution.py:47
  106.9 0.9 collective-permute-start.24
  108.2 3.5 %collective-permute-done.25 = bf16[512,256]{1,0:T(8,128)(2,1)S(1)} collective-permute-done((bf16[512,256]{1,0:T(8,128)(2,1)S(1)}, bf16[512,256]{1,0:T(8,128)(2,1)S(1)}, u32[]{:S(2)}, u32[]{:S(2)}) %collective-permute-start.25) | collective-permute-done | bytes 262176 | tf_op jit(solution)/shard_map/ppermute | solution.py:47
  111.7 1.2 collective-permute-start.27
  113.3 0.8 collective-permute-start.26
  114.5 3.5 %collective-permute-done.27 = bf16[512,256]{1,0:T(8,128)(2,1)S(1)} collective-permute-done((bf16[512,256]{1,0:T(8,128)(2,1)S(1)}, bf16[512,256]{1,0:T(8,128)(2,1)S(1)}, u32[]{:S(2)}, u32[]{:S(2)}) %collective-permute-start.27) | collective-permute-done | bytes 262176 | tf_op jit(solution)/shard_map/ppermute | solution.py:47
  118.4 1.3 collective-permute-done.26
  121.7 1.9 %collective-permute-start.31 = (bf16[256,256]{1,0:T(8,128)(2,1)S(1)}, bf16[256,256]{1,0:T(8,128)(2,1)S(1)}, u32[]{:S(2)}, u32[]{:S(2)}) collective-permute-start(bf16[256,256]{1,0:T(8,128)(2,1)S(1)} %reshape.240), channel_id=1, source_target_pairs={{0,16},{8,24},{16,0},{24,8},{1,17},{9,25},{17,1},{25,9},{2,18},{10... | collective-permute-start | bytes 393224 | tf_op jit(solution)/shard_map/ppermute | solution.py:103
  124.9 2.4 %collective-permute-done.31 = bf16[256,256]{1,0:T(8,128)(2,1)S(1)} collective-permute-done((bf16[256,256]{1,0:T(8,128)(2,1)S(1)}, bf16[256,256]{1,0:T(8,128)(2,1)S(1)}, u32[]{:S(2)}, u32[]{:S(2)}) %collective-permute-start.31) | collective-permute-done | bytes 131104 | tf_op jit(solution)/shard_map/ppermute | solution.py:103
  127.6 1.9 %collective-permute-done.33 = bf16[256,256]{1,0:T(8,128)(2,1)S(1)} collective-permute-done((bf16[256,256]{1,0:T(8,128)(2,1)S(1)}, bf16[256,256]{1,0:T(8,128)(2,1)S(1)}, u32[]{:S(2)}, u32[]{:S(2)}) %collective-permute-start.33) | collective-permute-done | bytes 131104 | tf_op jit(solution)/shard_map/ppermute | solution.py:103
  129.8 1.0 fusion.22
  (78 shorter events, 12.3 us)
Async XLA Ops:
  1.7 15.0 %collective-permute-start = (bf16[512,256]{1,0:T(8,128)(2,1)S(1)}, bf16[512,256]{1,0:T(8,128)(2,1)S(1)}, u32[]{:S(2)}, u32[]{:S(2)}) collective-permute-start(bf16[512,256]{1,0:T(8,128)(2,1)S(1)} %get-tuple-element.16), channel_id=1, source_target_pairs={{0,2},{2,4},{4,6},{6,7},{7,5},{5,3},{3,1},{1,0},{8,10},{10,12},{12... | collective-permute-start | bytes 786440 | tf_op jit(solution)/shard_map/ppermute | solution.py:46
  4.8 10.0 %collective-permute-start.1 = (bf16[512,256]{1,0:T(8,128)(2,1)S(1)}, bf16[512,256]{1,0:T(8,128)(2,1)S(1)}, u32[]{:S(2)}, u32[]{:S(2)}) collective-permute-start(bf16[512,256]{1,0:T(8,128)(2,1)S(1)} %get-tuple-element.17), channel_id=1, source_target_pairs={{2,0},{4,2},{6,4},{7,6},{5,7},{3,5},{1,3},{0,1},{10,8},{12,10},{14... | collective-permute-start | bytes 786440 | tf_op jit(solution)/shard_map/ppermute | solution.py:47
  9.8 114.8 %collective-permute-start.30 = (s32[2,128]{1,0:T(2,128)S(1)}, s32[2,128]{1,0:T(2,128)S(1)}, u32[]{:S(2)}, u32[]{:S(2)}) collective-permute-start(s32[2,128]{1,0:T(2,128)S(1)} %broadcast_select_fusion.3), channel_id=1, source_target_pairs={{0,16},{8,24},{16,0},{24,8},{1,17},{9,25},{17,1},{25,9},{2,18},{10... | collective-permute-start | bytes 3080 | tf_op jit(solution)/shard_map/ppermute | solution.py:90
  11.9 115.7 %collective-permute-start.32 = (s32[2,128]{1,0:T(2,128)S(1)}, s32[2,128]{1,0:T(2,128)S(1)}, u32[]{:S(2)}, u32[]{:S(2)}) collective-permute-start(s32[2,128]{1,0:T(2,128)S(1)} %broadcast_select_fusion.2), channel_id=1, source_target_pairs={{0,24},{8,16},{16,8},{24,0},{1,25},{9,17},{17,9},{25,1},{2,26},{10... | collective-permute-start | bytes 3080 | tf_op jit(solution)/shard_map/ppermute | solution.py:90
  11.9 117.9 %collective-permute-start.28 = (s32[2,128]{1,0:T(2,128)S(1)}, s32[2,128]{1,0:T(2,128)S(1)}, u32[]{:S(2)}, u32[]{:S(2)}) collective-permute-start(s32[2,128]{1,0:T(2,128)S(1)} %broadcast_select_fusion.4), channel_id=1, source_target_pairs={{0,8},{8,0},{16,24},{24,16},{1,9},{9,1},{17,25},{25,17},{2,10},{10... | collective-permute-start | bytes 3080 | tf_op jit(solution)/shard_map/ppermute | solution.py:90
  12.2 20.0 %copy-start = (bf16[1,1024,8192]{2,1,0:T(8,128)(2,1)S(1)}, bf16[1,1024,8192]{2,1,0:T(8,128)(2,1)}, u32[]{:S(2)}) copy-start(bf16[1,1024,8192]{2,1,0:T(8,128)(2,1)} %param.7) | copy-start | bytes 50331652
  14.8 8.4 %collective-permute-start.3 = (bf16[512,256]{1,0:T(8,128)(2,1)S(1)}, bf16[512,256]{1,0:T(8,128)(2,1)S(1)}, u32[]{:S(2)}, u32[]{:S(2)}) collective-permute-start(bf16[512,256]{1,0:T(8,128)(2,1)S(1)} %collective-permute-done.1), channel_id=1, source_target_pairs={{2,0},{4,2},{6,4},{7,6},{5,7},{3,5},{1,3},{0,1},{10,8},{12,10},{14... | collective-permute-start | bytes 786440 | tf_op jit(solution)/shard_map/ppermute | solution.py:47
  16.7 9.9 %collective-permute-start.2 = (bf16[512,256]{1,0:T(8,128)(2,1)S(1)}, bf16[512,256]{1,0:T(8,128)(2,1)S(1)}, u32[]{:S(2)}, u32[]{:S(2)}) collective-permute-start(bf16[512,256]{1,0:T(8,128)(2,1)S(1)} %collective-permute-done), channel_id=1, source_target_pairs={{0,2},{2,4},{4,6},{6,7},{7,5},{5,3},{3,1},{1,0},{8,10},{10,12},{12... | collective-permute-start | bytes 786440 | tf_op jit(solution)/shard_map/ppermute | solution.py:46
  23.3 7.6 %collective-permute-start.5 = (bf16[512,256]{1,0:T(8,128)(2,1)S(1)}, bf16[512,256]{1,0:T(8,128)(2,1)S(1)}, u32[]{:S(2)}, u32[]{:S(2)}) collective-permute-start(bf16[512,256]{1,0:T(8,128)(2,1)S(1)} %collective-permute-done.3), channel_id=1, source_target_pairs={{2,0},{4,2},{6,4},{7,6},{5,7},{3,5},{1,3},{0,1},{10,8},{12,10},{14... | collective-permute-start | bytes 786440 | tf_op jit(solution)/shard_map/ppermute | solution.py:47
  26.6 7.1 %collective-permute-start.4 = (bf16[512,256]{1,0:T(8,128)(2,1)S(1)}, bf16[512,256]{1,0:T(8,128)(2,1)S(1)}, u32[]{:S(2)}, u32[]{:S(2)}) collective-permute-start(bf16[512,256]{1,0:T(8,128)(2,1)S(1)} %collective-permute-done.2), channel_id=1, source_target_pairs={{0,2},{2,4},{4,6},{6,7},{7,5},{5,3},{3,1},{1,0},{8,10},{10,12},{12... | collective-permute-start | bytes 786440 | tf_op jit(solution)/shard_map/ppermute | solution.py:46
  30.8 6.6 %collective-permute-start.7 = (bf16[512,256]{1,0:T(8,128)(2,1)S(1)}, bf16[512,256]{1,0:T(8,128)(2,1)S(1)}, u32[]{:S(2)}, u32[]{:S(2)}) collective-permute-start(bf16[512,256]{1,0:T(8,128)(2,1)S(1)} %collective-permute-done.5), channel_id=1, source_target_pairs={{2,0},{4,2},{6,4},{7,6},{5,7},{3,5},{1,3},{0,1},{10,8},{12,10},{14... | collective-permute-start | bytes 786440 | tf_op jit(solution)/shard_map/ppermute | solution.py:47
  33.7 6.6 %collective-permute-start.6 = (bf16[512,256]{1,0:T(8,128)(2,1)S(1)}, bf16[512,256]{1,0:T(8,128)(2,1)S(1)}, u32[]{:S(2)}, u32[]{:S(2)}) collective-permute-start(bf16[512,256]{1,0:T(8,128)(2,1)S(1)} %collective-permute-done.4), channel_id=1, source_target_pairs={{0,2},{2,4},{4,6},{6,7},{7,5},{5,3},{3,1},{1,0},{8,10},{10,12},{12... | collective-permute-start | bytes 786440 | tf_op jit(solution)/shard_map/ppermute | solution.py:46
  37.5 7.1 %collective-permute-start.9 = (bf16[512,256]{1,0:T(8,128)(2,1)S(1)}, bf16[512,256]{1,0:T(8,128)(2,1)S(1)}, u32[]{:S(2)}, u32[]{:S(2)}) collective-permute-start(bf16[512,256]{1,0:T(8,128)(2,1)S(1)} %collective-permute-done.7), channel_id=1, source_target_pairs={{2,0},{4,2},{6,4},{7,6},{5,7},{3,5},{1,3},{0,1},{10,8},{12,10},{14... | collective-permute-start | bytes 786440 | tf_op jit(solution)/shard_map/ppermute | solution.py:47
  39.5 27.8 %slice-start = ((s8[12582912]{0:T(1024)(128)(4,1)}), s8[4194304]{0:T(1024)(128)(4,1)S(1)}, s32[]{:S(2)}) async-start(s8[12582912]{0:T(1024)(128)(4,1)} %bitcast.153), calls=%async_computation | async-start | bytes 8388608
  40.4 7.4 %collective-permute-start.8 = (bf16[512,256]{1,0:T(8,128)(2,1)S(1)}, bf16[512,256]{1,0:T(8,128)(2,1)S(1)}, u32[]{:S(2)}, u32[]{:S(2)}) collective-permute-start(bf16[512,256]{1,0:T(8,128)(2,1)S(1)} %collective-permute-done.6), channel_id=1, source_target_pairs={{0,2},{2,4},{4,6},{6,7},{7,5},{5,3},{3,1},{1,0},{8,10},{10,12},{12... | collective-permute-start | bytes 786440 | tf_op jit(solution)/shard_map/ppermute | solution.py:46
  44.6 7.9 %collective-permute-start.11 = (bf16[512,256]{1,0:T(8,128)(2,1)S(1)}, bf16[512,256]{1,0:T(8,128)(2,1)S(1)}, u32[]{:S(2)}, u32[]{:S(2)}) collective-permute-start(bf16[512,256]{1,0:T(8,128)(2,1)S(1)} %collective-permute-done.9), channel_id=1, source_target_pairs={{2,0},{4,2},{6,4},{7,6},{5,7},{3,5},{1,3},{0,1},{10,8},{12,10},{14... | collective-permute-start | bytes 786440 | tf_op jit(solution)/shard_map/ppermute | solution.py:47
  47.0 20.4 %slice-start.1 = ((s8[12582912]{0:T(1024)(128)(4,1)}), s8[4194304]{0:T(1024)(128)(4,1)S(1)}, s32[]{:S(2)}) async-start(s8[12582912]{0:T(1024)(128)(4,1)} %bitcast.153), calls=%async_computation.1 | async-start | bytes 8388608
  47.8 8.3 %collective-permute-start.10 = (bf16[512,256]{1,0:T(8,128)(2,1)S(1)}, bf16[512,256]{1,0:T(8,128)(2,1)S(1)}, u32[]{:S(2)}, u32[]{:S(2)}) collective-permute-start(bf16[512,256]{1,0:T(8,128)(2,1)S(1)} %collective-permute-done.8), channel_id=1, source_target_pairs={{0,2},{2,4},{4,6},{6,7},{7,5},{5,3},{3,1},{1,0},{8,10},{10,12},{12... | collective-permute-start | bytes 786440 | tf_op jit(solution)/shard_map/ppermute | solution.py:46
  52.5 6.6 %collective-permute-start.13 = (bf16[512,256]{1,0:T(8,128)(2,1)S(1)}, bf16[512,256]{1,0:T(8,128)(2,1)S(1)}, u32[]{:S(2)}, u32[]{:S(2)}) collective-permute-start(bf16[512,256]{1,0:T(8,128)(2,1)S(1)} %collective-permute-done.11), channel_id=1, source_target_pairs={{2,0},{4,2},{6,4},{7,6},{5,7},{3,5},{1,3},{0,1},{10,8},{12,10},{14... | collective-permute-start | bytes 786440 | tf_op jit(solution)/shard_map/ppermute | solution.py:47
  55.3 12.0 %slice-start.2 = ((s8[12582912]{0:T(1024)(128)(4,1)}), s8[4194304]{0:T(1024)(128)(4,1)S(1)}, s32[]{:S(2)}) async-start(s8[12582912]{0:T(1024)(128)(4,1)} %bitcast.153), calls=%async_computation.2 | async-start | bytes 8388608
  56.0 8.6 %collective-permute-start.12 = (bf16[512,256]{1,0:T(8,128)(2,1)S(1)}, bf16[512,256]{1,0:T(8,128)(2,1)S(1)}, u32[]{:S(2)}, u32[]{:S(2)}) collective-permute-start(bf16[512,256]{1,0:T(8,128)(2,1)S(1)} %collective-permute-done.10), channel_id=1, source_target_pairs={{0,2},{2,4},{4,6},{6,7},{7,5},{5,3},{3,1},{1,0},{8,10},{10,12},{12... | collective-permute-start | bytes 786440 | tf_op jit(solution)/shard_map/ppermute | solution.py:46
  65.1 41.8 %copy-start.1 = (bf16[1024,256]{1,0:T(8,128)(2,1)}, bf16[1024,256]{1,0:T(8,128)(2,1)S(1)}, u32[]{:S(2)}) copy-start(bf16[1024,256]{1,0:T(8,128)(2,1)S(1)} %fusion.12) | copy-start | bytes 1572868
  65.2 8.1 %collective-permute-start.14 = (bf16[512,256]{1,0:T(8,128)(2,1)S(1)}, bf16[512,256]{1,0:T(8,128)(2,1)S(1)}, u32[]{:S(2)}, u32[]{:S(2)}) collective-permute-start(bf16[512,256]{1,0:T(8,128)(2,1)S(1)} %get-tuple-element.14), channel_id=1, source_target_pairs={{0,2},{2,4},{4,6},{6,7},{7,5},{5,3},{3,1},{1,0},{8,10},{10,12},{12... | collective-permute-start | bytes 786440 | tf_op jit(solution)/shard_map/ppermute | solution.py:46
  65.3 8.6 %collective-permute-start.15 = (bf16[512,256]{1,0:T(8,128)(2,1)S(1)}, bf16[512,256]{1,0:T(8,128)(2,1)S(1)}, u32[]{:S(2)}, u32[]{:S(2)}) collective-permute-start(bf16[512,256]{1,0:T(8,128)(2,1)S(1)} %get-tuple-element.15), channel_id=1, source_target_pairs={{2,0},{4,2},{6,4},{7,6},{5,7},{3,5},{1,3},{0,1},{10,8},{12,10},{14... | collective-permute-start | bytes 786440 | tf_op jit(solution)/shard_map/ppermute | solution.py:47
  73.3 9.8 %collective-permute-start.16 = (bf16[512,256]{1,0:T(8,128)(2,1)S(1)}, bf16[512,256]{1,0:T(8,128)(2,1)S(1)}, u32[]{:S(2)}, u32[]{:S(2)}) collective-permute-start(bf16[512,256]{1,0:T(8,128)(2,1)S(1)} %collective-permute-done.14), channel_id=1, source_target_pairs={{0,2},{2,4},{4,6},{6,7},{7,5},{5,3},{3,1},{1,0},{8,10},{10,12},{12... | collective-permute-start | bytes 786440 | tf_op jit(solution)/shard_map/ppermute | solution.py:46
  73.9 7.5 %collective-permute-start.17 = (bf16[512,256]{1,0:T(8,128)(2,1)S(1)}, bf16[512,256]{1,0:T(8,128)(2,1)S(1)}, u32[]{:S(2)}, u32[]{:S(2)}) collective-permute-start(bf16[512,256]{1,0:T(8,128)(2,1)S(1)} %collective-permute-done.15), channel_id=1, source_target_pairs={{2,0},{4,2},{6,4},{7,6},{5,7},{3,5},{1,3},{0,1},{10,8},{12,10},{14... | collective-permute-start | bytes 786440 | tf_op jit(solution)/shard_map/ppermute | solution.py:47
  81.4 6.5 %collective-permute-start.19 = (bf16[512,256]{1,0:T(8,128)(2,1)S(1)}, bf16[512,256]{1,0:T(8,128)(2,1)S(1)}, u32[]{:S(2)}, u32[]{:S(2)}) collective-permute-start(bf16[512,256]{1,0:T(8,128)(2,1)S(1)} %collective-permute-done.17), channel_id=1, source_target_pairs={{2,0},{4,2},{6,4},{7,6},{5,7},{3,5},{1,3},{0,1},{10,8},{12,10},{14... | collective-permute-start | bytes 786440 | tf_op jit(solution)/shard_map/ppermute | solution.py:47
  83.1 7.4 %collective-permute-start.18 = (bf16[512,256]{1,0:T(8,128)(2,1)S(1)}, bf16[512,256]{1,0:T(8,128)(2,1)S(1)}, u32[]{:S(2)}, u32[]{:S(2)}) collective-permute-start(bf16[512,256]{1,0:T(8,128)(2,1)S(1)} %collective-permute-done.16), channel_id=1, source_target_pairs={{0,2},{2,4},{4,6},{6,7},{7,5},{5,3},{3,1},{1,0},{8,10},{10,12},{12... | collective-permute-start | bytes 786440 | tf_op jit(solution)/shard_map/ppermute | solution.py:46
  87.9 7.5 %collective-permute-start.21 = (bf16[512,256]{1,0:T(8,128)(2,1)S(1)}, bf16[512,256]{1,0:T(8,128)(2,1)S(1)}, u32[]{:S(2)}, u32[]{:S(2)}) collective-permute-start(bf16[512,256]{1,0:T(8,128)(2,1)S(1)} %collective-permute-done.19), channel_id=1, source_target_pairs={{2,0},{4,2},{6,4},{7,6},{5,7},{3,5},{1,3},{0,1},{10,8},{12,10},{14... | collective-permute-start | bytes 786440 | tf_op jit(solution)/shard_map/ppermute | solution.py:47
  90.5 7.5 %collective-permute-start.20 = (bf16[512,256]{1,0:T(8,128)(2,1)S(1)}, bf16[512,256]{1,0:T(8,128)(2,1)S(1)}, u32[]{:S(2)}, u32[]{:S(2)}) collective-permute-start(bf16[512,256]{1,0:T(8,128)(2,1)S(1)} %collective-permute-done.18), channel_id=1, source_target_pairs={{0,2},{2,4},{4,6},{6,7},{7,5},{5,3},{3,1},{1,0},{8,10},{10,12},{12... | collective-permute-start | bytes 786440 | tf_op jit(solution)/shard_map/ppermute | solution.py:46
  91.4 32.5 %copy-start.2 = (bf16[1,512,256]{2,1,0:T(8,128)(2,1)S(1)}, bf16[1,512,256]{2,1,0:T(8,128)(2,1)}, u32[]{:S(2)}) copy-start(bf16[1,512,256]{2,1,0:T(8,128)(2,1)} %param.13) | copy-start | bytes 786436
  95.4 9.1 %collective-permute-start.23 = (bf16[512,256]{1,0:T(8,128)(2,1)S(1)}, bf16[512,256]{1,0:T(8,128)(2,1)S(1)}, u32[]{:S(2)}, u32[]{:S(2)}) collective-permute-start(bf16[512,256]{1,0:T(8,128)(2,1)S(1)} %collective-permute-done.21), channel_id=1, source_target_pairs={{2,0},{4,2},{6,4},{7,6},{5,7},{3,5},{1,3},{0,1},{10,8},{12,10},{14... | collective-permute-start | bytes 786440 | tf_op jit(solution)/shard_map/ppermute | solution.py:47
  97.9 9.0 %collective-permute-start.22 = (bf16[512,256]{1,0:T(8,128)(2,1)S(1)}, bf16[512,256]{1,0:T(8,128)(2,1)S(1)}, u32[]{:S(2)}, u32[]{:S(2)}) collective-permute-start(bf16[512,256]{1,0:T(8,128)(2,1)S(1)} %collective-permute-done.20), channel_id=1, source_target_pairs={{0,2},{2,4},{4,6},{6,7},{7,5},{5,3},{3,1},{1,0},{8,10},{10,12},{12... | collective-permute-start | bytes 786440 | tf_op jit(solution)/shard_map/ppermute | solution.py:46
  104.5 7.2 %collective-permute-start.25 = (bf16[512,256]{1,0:T(8,128)(2,1)S(1)}, bf16[512,256]{1,0:T(8,128)(2,1)S(1)}, u32[]{:S(2)}, u32[]{:S(2)}) collective-permute-start(bf16[512,256]{1,0:T(8,128)(2,1)S(1)} %collective-permute-done.23), channel_id=1, source_target_pairs={{2,0},{4,2},{6,4},{7,6},{5,7},{3,5},{1,3},{0,1},{10,8},{12,10},{14... | collective-permute-start | bytes 786440 | tf_op jit(solution)/shard_map/ppermute | solution.py:47
  106.9 6.4 %collective-permute-start.24 = (bf16[512,256]{1,0:T(8,128)(2,1)S(1)}, bf16[512,256]{1,0:T(8,128)(2,1)S(1)}, u32[]{:S(2)}, u32[]{:S(2)}) collective-permute-start(bf16[512,256]{1,0:T(8,128)(2,1)S(1)} %collective-permute-done.22), channel_id=1, source_target_pairs={{0,2},{2,4},{4,6},{6,7},{7,5},{5,3},{3,1},{1,0},{8,10},{10,12},{12... | collective-permute-start | bytes 786440 | tf_op jit(solution)/shard_map/ppermute | solution.py:46
  111.7 6.4 %collective-permute-start.27 = (bf16[512,256]{1,0:T(8,128)(2,1)S(1)}, bf16[512,256]{1,0:T(8,128)(2,1)S(1)}, u32[]{:S(2)}, u32[]{:S(2)}) collective-permute-start(bf16[512,256]{1,0:T(8,128)(2,1)S(1)} %collective-permute-done.25), channel_id=1, source_target_pairs={{2,0},{4,2},{6,4},{7,6},{5,7},{3,5},{1,3},{0,1},{10,8},{12,10},{14... | collective-permute-start | bytes 786440 | tf_op jit(solution)/shard_map/ppermute | solution.py:47
  113.3 6.4 %collective-permute-start.26 = (bf16[512,256]{1,0:T(8,128)(2,1)S(1)}, bf16[512,256]{1,0:T(8,128)(2,1)S(1)}, u32[]{:S(2)}, u32[]{:S(2)}) collective-permute-start(bf16[512,256]{1,0:T(8,128)(2,1)S(1)} %collective-permute-done.24), channel_id=1, source_target_pairs={{0,2},{2,4},{4,6},{6,7},{7,5},{5,3},{3,1},{1,0},{8,10},{10,12},{12... | collective-permute-start | bytes 786440 | tf_op jit(solution)/shard_map/ppermute | solution.py:46
  121.7 5.7 %collective-permute-start.31 = (bf16[256,256]{1,0:T(8,128)(2,1)S(1)}, bf16[256,256]{1,0:T(8,128)(2,1)S(1)}, u32[]{:S(2)}, u32[]{:S(2)}) collective-permute-start(bf16[256,256]{1,0:T(8,128)(2,1)S(1)} %reshape.240), channel_id=1, source_target_pairs={{0,16},{8,24},{16,0},{24,8},{1,17},{9,25},{17,1},{25,9},{2,18},{10... | collective-permute-start | bytes 393224 | tf_op jit(solution)/shard_map/ppermute | solution.py:103
  123.8 5.7 %collective-permute-start.33 = (bf16[256,256]{1,0:T(8,128)(2,1)S(1)}, bf16[256,256]{1,0:T(8,128)(2,1)S(1)}, u32[]{:S(2)}, u32[]{:S(2)}) collective-permute-start(bf16[256,256]{1,0:T(8,128)(2,1)S(1)} %reshape.241), channel_id=1, source_target_pairs={{0,24},{8,16},{16,8},{24,0},{1,25},{9,17},{17,9},{25,1},{2,26},{10... | collective-permute-start | bytes 393224 | tf_op jit(solution)/shard_map/ppermute | solution.py:103
  124.6 5.2 %collective-permute-start.29 = (bf16[256,256]{1,0:T(8,128)(2,1)S(1)}, bf16[256,256]{1,0:T(8,128)(2,1)S(1)}, u32[]{:S(2)}, u32[]{:S(2)}) collective-permute-start(bf16[256,256]{1,0:T(8,128)(2,1)S(1)} %reshape.239), channel_id=1, source_target_pairs={{0,8},{8,0},{16,24},{24,16},{1,9},{9,1},{17,25},{25,17},{2,10},{10... | collective-permute-start | bytes 393224 | tf_op jit(solution)/shard_map/ppermute | solution.py:103
